TPU v7x, 32 devices: a whole 2x2x4 slice. The times are simulated.
32 devices in a mesh: gx: 8 (over z, y), gy: 4 (over x, core).
Axes of the slice: x: 2, y: 2, z: 4, core: 2. Of those that a mesh axis runs over, the one named last changes fastest.
Arguments:
- adjoint_state: float32 [5, 16, 128, 512], P(None, None, 'gx', 'gy'), may hold values from -6 to 6
- trajectory: float32 [2, 5, 16, 128, 512], P(None, None, None, 'gx', 'gy'), may hold values from -3 to 3
- ray_resid: float32 [16384, 2, 128], P(('gx', 'gy')), may hold values from -6 to 6
- ray_angle: float32 [16384, 128], P(('gx', 'gy')), may hold values from -3.140625 to 3.140625
- ray_slope: float32 [16384, 128], P(('gx', 'gy')), may hold values from 0.5 to 4
- ray_dest: int32 [16384, 1], P(('gx', 'gy')), may hold values from 0 to 31; in each aligned block of 512 rows (0 to 511, 512 to 1023, ...) at most 32 rows name the same one
- gate_cell: int32 [16384, 128], P(('gx', 'gy')), may hold values from 0 to 32767
Outputs:
- initial_grad: float32 [5, 16, 128, 512], P(None, None, 'gx', 'gy')
Inputs may be any that keep to these rules, and one draw needn't show every extreme that they name: `ray_dest`: each aligned block of 512 ray groups (the ray groups of one device) names any one tile at most 32 times; some tile is named exactly 32 times.
All inputs are finite; a program needn't handle non-finite values.
Results may differ from a plain program's by a relative error of at most 0.00002.
Values sent between devices are 32-bit elements; how exact they have to be, the bound alone decides.
A program may use at most 192 MiB of HBM per device.

v0:
```python
import jax
import jax.numpy as jnp
from jax import lax
from jax.sharding import PartitionSpec as P

diffusion = 0.1
latent = 2.0


def with_halo(block, sides, width):
    for axis, dim in sides:
        count = lax.axis_size(axis)
        forward = [(i, i + 1) for i in range(count - 1)]
        backward = [(target, source) for source, target in forward]
        low = lax.ppermute(
            lax.slice_in_dim(block, block.shape[dim] - width, None, axis=dim), axis, forward
        )
        high = lax.ppermute(lax.slice_in_dim(block, 0, width, axis=dim), axis, backward)
        block = jnp.concatenate([low, block, high], axis=dim)
    return block


def f_valid(state_pad, traj_pad):
    center = state_pad[..., 1:-1, 1:-1]
    diff_x = 0.5 * (state_pad[..., 2:, 1:-1] - state_pad[..., :-2, 1:-1])
    diff_y = 0.5 * (state_pad[..., 1:-1, 2:] - state_pad[..., 1:-1, :-2])
    laplace = (
        state_pad[..., 2:, 1:-1]
        + state_pad[..., :-2, 1:-1]
        + state_pad[..., 1:-1, 2:]
        + state_pad[..., 1:-1, :-2]
        - 4.0 * center
    )
    grad_x = 0.5 * (traj_pad[..., 2:, 1:-1] - traj_pad[..., :-2, 1:-1])
    grad_y = 0.5 * (traj_pad[..., 1:-1, 2:] - traj_pad[..., 1:-1, :-2])
    wind_u = traj_pad[0, :, 1:-1, 1:-1]
    wind_v = traj_pad[1, :, 1:-1, 1:-1]
    advected = (
        center
        - (wind_u * diff_x + wind_v * diff_y)
        - (center[0] * grad_x + center[1] * grad_y)
        + diffusion * laplace
    )
    convert = 0.3 * jax.nn.sigmoid(traj_pad[2, :, 1:-1, 1:-1])
    falling = 0.3 * jax.nn.sigmoid(traj_pad[4, :, 1:-1, 1:-1])
    condensed = convert * advected[3]
    rain_old = advected[4]
    from_above = jnp.concatenate([rain_old[1:], jnp.zeros_like(rain_old[:1])], axis=0)
    rain_new = rain_old + condensed + falling * (from_above - rain_old)
    return jnp.stack(
        [
            advected[0],
            advected[1],
            advected[2] + latent * condensed,
            advected[3] - condensed,
            rain_new,
        ]
    )


def adjoint_region(cot_ext, traj_ext):
    primal = jnp.zeros_like(traj_ext)
    unused, pullback = jax.vjp(lambda state_pad: f_valid(state_pad, traj_ext), primal)
    cotangent = pullback(cot_ext)[0]
    return cotangent[..., 2:-2, 2:-2]


def local(adjoint_state, trajectory, ray_resid, ray_angle, ray_slope, ray_dest, gate_cell):
    tiles_x = lax.axis_size("gx")
    tiles_y = lax.axis_size("gy")
    devices = tiles_x * tiles_y
    ray_count = ray_resid.shape[0]
    gate_count = ray_resid.shape[2]
    capacity = max(2, 2 * ray_count // devices)
    velocity = ray_resid[:, 0]
    contrib = jnp.stack(
        [jnp.sin(ray_angle) * velocity, jnp.cos(ray_angle) * velocity, ray_slope * ray_resid[:, 1]],
        axis=1,
    )
    target = ray_dest[:, 0]
    positions = jnp.arange(ray_count, dtype=jnp.int32)
    earlier = (target[:, None] == target[None, :]) & (positions[None, :] < positions[:, None])
    slot_rank = jnp.sum(earlier.astype(jnp.int32), axis=1)
    slot_index = target * capacity + slot_rank
    slots_total = devices * capacity
    slot_ids = jnp.arange(slots_total, dtype=jnp.int32)
    matches = slot_index[None, :] == slot_ids[:, None]
    filled = jnp.any(matches, axis=1)
    source = jnp.sum(jnp.where(matches, positions[None, :], 0), axis=1)
    values = jnp.take(contrib, source, axis=0) * filled.astype(jnp.float32)[:, None, None]
    cell_index = jnp.where(filled[:, None], jnp.take(gate_cell, source, axis=0), 0)
    got_values, got_cells = (
        lax.all_to_all(
            values.reshape(devices, capacity, 3, gate_count),
            ("gx", "gy"),
            split_axis=0,
            concat_axis=0,
            tiled=True,
        ),
        lax.all_to_all(
            cell_index.reshape(devices, capacity, gate_count),
            ("gx", "gy"),
            split_axis=0,
            concat_axis=0,
            tiled=True,
        ),
    )
    levels = adjoint_state.shape[1]
    cols_x = adjoint_state.shape[2]
    cols_y = adjoint_state.shape[3]
    flat_values = jnp.transpose(got_values.reshape(-1, 3, gate_count), (1, 0, 2)).reshape(3, -1)
    flat_cells = got_cells.reshape(-1).astype(jnp.int32)
    forcing = (
        jnp.zeros((3, levels * cols_x * cols_y), jnp.float32).at[:, flat_cells].add(flat_values)
    )
    forcing = forcing.reshape(3, levels, cols_x, cols_y)
    blank_field = jnp.zeros_like(forcing[0])
    result = adjoint_state + jnp.stack(
        [forcing[0], forcing[1], blank_field, blank_field, forcing[2]]
    )
    rim_width = 2
    traj_ext = with_halo(trajectory, (("gx", 3), ("gy", 4)), rim_width)
    for section in (1, 0):
        extended = with_halo(result, (("gx", 2), ("gy", 3)), 1)
        result = adjoint_region(extended, traj_ext[section])
    return result


def solution(mesh):
    return jax.shard_map(
        local,
        mesh=mesh,
        in_specs=(
            P(None, None, "gx", "gy"),
            P(None, None, None, "gx", "gy"),
            P(("gx", "gy"), None, None),
            P(("gx", "gy"), None),
            P(("gx", "gy"), None),
            P(("gx", "gy"), None),
            P(("gx", "gy"), None),
        ),
        out_specs=P(None, None, "gx", "gy"),
        check_vma=False,
    )
```

profile of v0, /device:TPU:18, one launch (start us, length us, event | category | flops | bytes accessed | tf_op | source)
XLA Modules:
  0.0 1106.7 jit_solution(13801527991847494200)
XLA Ops:
  2.5 2.8 gather_fusion
  5.3 1.1 select_select_fusion
  6.4 6.0 all-to-all-start
  13.2 3.4 collective-permute-start.4
  17.3 3.3 collective-permute-start.5
  22.1 5.5 copy.80
  28.3 3.6 gather_fusion.1
  31.9 6.3 copy.79
  38.2 6.4 copy.81
  44.6 12.2 %pad_maximum_fusion = f32[2,5,16,20,128]{3,2,4,1,0:T(8,128)S(1)} fusion(f32[2,5,16,2,128]{3,2,4,1,0:T(8,128)} %copy.81, f32[2,5,16,16,128]{3,2,4,1,0:T(8,128)} %copy.80, f32[2,5,16,2,128]{3,2,4,1,0:T(8,128)} %copy.79), kind=kLoop, calls=%fused_computation.6 | loop fusion | flops 819200 | bytes 3276800 | tf_op jit(solution)/shard_map/concatenate | solution.py:19
  56.8 4.0 copy-done.2
  60.7 1.9 collective-permute-start.6
  62.7 3.6 collective-permute-start.7
  66.3 1.5 fusion.3
  67.9 7.0 copy.83
  74.9 2.1 copy.82
  77.0 2.1 copy.84
  79.1 6.0 all-to-all-start.1
  85.1 2.4 compare_select_fusion
  87.5 33.1 %all-to-all-done.1 = f32[32,32,3,128]{3,1,2,0:T(8,128)} async-done(((f32[32,32,3,128]{3,1,2,0:T(8,128)}), f32[32,32,3,128]{3,1,2,0:T(8,128)}, u32[]{:S(2)}, u32[]{:S(2)}) %all-to-all-start.1) | async-done | bytes 1572896 | tf_op jit(solution)/shard_map/all_to_all | solution.py:93
  120.5 2.7 copy.69
  123.3 31.1 %copy.90 = f32[3,1024,128]{0,2,1:T(8,128)} copy(f32[3,1024,128]{2,1,0:T(8,128)} %bitcast.72) | data formatting | bytes 3145728 | tf_op jit(solution)/shard_map/reshape | solution.py:111
  154.4 760.0 %scatter_custom_fusion = f32[3,32768]{0,1:T(8,128)} fusion(s32[131072]{0:T(1024)} %bitcast.88, f32[131072,3]{1,0:T(8,128)} %bitcast.16, f32[]{:T(128)} %constant.16.clone.1), kind=kCustom, calls=%fused_computation.7 | custom fusion | flops 393216 | bytes 393728 | tf_op jit(solution)/shard_map/scatter-add | solution.py:114
  914.4 30.5 %slice_reduce_fusion.2 = (f32[32768]{0:T(1024)S(1)}, f32[32768]{0:T(1024)S(1)}, f32[32768]{0:T(1024)S(1)}) fusion(f32[3,32768]{0,1:T(8,128)} %scatter_custom_fusion), kind=kLoop, calls=%fused_computation.5 | loop fusion | bytes 786432 | tf_op jit(solution)/shard_map/slice | solution.py:119
  946.4 1.9 collective-permute-start
  948.3 102.7 %collective-permute-start.1 = (f32[5,16,1,128]{3,1,2,0:T(8,128)S(1)}, f32[5,16,1,128]{3,1,2,0:T(8,128)S(1)}, u32[]{:S(2)}, u32[]{:S(2)}) collective-permute-start(f32[5,16,1,128]{3,1,2,0:T(8,128)S(1)} %get-tuple-element.55), channel_id=1, source_target_pairs={{4,0},{8,4},{12,8},{16,12},{20,16},{24,20},{28,24},{5,1},{9,5},{13... | collective-permute-start | bytes 122888 | tf_op jit(solution)/shard_map/ppermute | solution.py:18
  1051.1 3.0 pad_maximum_fusion.1
  1055.0 3.1 collective-permute-start.2
  1058.7 2.4 collective-permute-start.3
  1061.1 2.5 slice_bitcast_fusion.1
  1063.6 1.5 copy.75
  1065.1 1.5 copy.76
  1066.6 2.2 pad_maximum_fusion.2
  1071.3 1.2 fusion.15
  1072.5 1.0 fusion.45
  1073.5 2.7 pad_add_fusion.1
  1076.3 2.1 collective-permute-start.8
  1078.4 4.7 collective-permute-start.9
  1083.3 1.4 collective-permute-done.9
  1084.8 1.2 fusion.50
  1086.0 1.7 copy.97
  1087.7 1.9 collective-permute-start.10
  1090.2 3.9 collective-permute-start.11
  1095.5 1.5 copy.88
  1096.9 1.8 pad_maximum_fusion.3
  1101.0 1.2 fusion.9
  1103.0 1.1 fusion.43
  1104.2 1.1 pad_add_fusion.4
  (83 shorter events, 18.1 us)
Async XLA Ops:
  0.0 2.5 copy-start
  5.3 7.1 copy-start.9
  5.3 15.4 %copy-start.11 = (f32[512,2,128]{2,1,0:T(2,128)S(1)}, f32[512,2,128]{2,1,0:T(2,128)}, u32[]{:S(2)}) copy-start(f32[512,2,128]{2,1,0:T(2,128)} %param.9) | copy-start | bytes 1572868
  6.4 14.7 %copy-start.13 = (f32[512,128]{1,0:T(8,128)S(1)}, f32[512,128]{1,0:T(8,128)}, u32[]{:S(2)}) copy-start(f32[512,128]{1,0:T(8,128)} %param.10) | copy-start | bytes 786436
  6.4 72.6 %all-to-all-start = ((s32[32,32,128]{2,1,0:T(8,128)}), s32[32,32,128]{2,1,0:T(8,128)}, u32[]{:S(2)}, u32[]{:S(2)}) async-start(s32[32,32,128]{2,1,0:T(8,128)} %select_select_fusion), calls=%async_computation | async-start | bytes 1048576 | tf_op jit(solution)/shard_map/all_to_all | solution.py:100
  13.2 18.7 %collective-permute-start.4 = (f32[2,5,16,2,128]{4,2,3,1,0:T(8,128)}, f32[2,5,16,2,128]{4,2,3,1,0:T(8,128)}, u32[]{:S(2)}, u32[]{:S(2)}) collective-permute-start(f32[2,5,16,2,128]{4,2,3,1,0:T(8,128)} %copy.95), channel_id=1, source_target_pairs={{0,4},{4,8},{8,12},{12,16},{16,20},{20,24},{24,28},{1,5},{5,9},{9,... | collective-permute-start | bytes 491528 | tf_op jit(solution)/shard_map/ppermute | solution.py:15
  17.3 20.8 %collective-permute-start.5 = (f32[2,5,16,2,128]{4,2,3,1,0:T(8,128)}, f32[2,5,16,2,128]{4,2,3,1,0:T(8,128)}, u32[]{:S(2)}, u32[]{:S(2)}) collective-permute-start(f32[2,5,16,2,128]{4,2,3,1,0:T(8,128)} %copy.96), channel_id=1, source_target_pairs={{4,0},{8,4},{12,8},{16,12},{20,16},{24,20},{28,24},{5,1},{9,5},{13... | collective-permute-start | bytes 491528 | tf_op jit(solution)/shard_map/ppermute | solution.py:18
  22.1 5.5 copy-start.12
  56.7 4.0 copy-start.2
  60.7 14.2 %collective-permute-start.6 = (f32[2,5,16,20,2]{3,2,4,1,0:T(8,128)S(1)}, f32[2,5,16,20,2]{3,2,4,1,0:T(8,128)}, u32[]{:S(2)}, u32[]{:S(2)}) collective-permute-start(f32[2,5,16,20,2]{3,2,4,1,0:T(8,128)S(1)} %get-tuple-element.24), channel_id=1, source_target_pairs={{0,1},{1,2},{2,3},{4,5},{5,6},{6,7},{8,9},{9,10},{10,11},{12,13},{... | collective-permute-start | bytes 76808 | tf_op jit(solution)/shard_map/ppermute | solution.py:15
  62.7 14.3 %collective-permute-start.7 = (f32[2,5,16,20,2]{3,2,4,1,0:T(8,128)S(1)}, f32[2,5,16,20,2]{3,2,4,1,0:T(8,128)}, u32[]{:S(2)}, u32[]{:S(2)}) collective-permute-start(f32[2,5,16,20,2]{3,2,4,1,0:T(8,128)S(1)} %get-tuple-element.25), channel_id=1, source_target_pairs={{1,0},{2,1},{3,2},{5,4},{6,5},{7,6},{9,8},{10,9},{11,10},{13,12},{... | collective-permute-start | bytes 76808 | tf_op jit(solution)/shard_map/ppermute | solution.py:18
  79.1 41.4 %all-to-all-start.1 = ((f32[32,32,3,128]{3,1,2,0:T(8,128)}), f32[32,32,3,128]{3,1,2,0:T(8,128)}, u32[]{:S(2)}, u32[]{:S(2)}) async-start(f32[32,32,3,128]{3,1,2,0:T(8,128)} %fusion.3), calls=%async_computation.1 | async-start | bytes 3145728 | tf_op jit(solution)/shard_map/all_to_all | solution.py:93
  944.9 1.1 copy-start.10
  944.9 106.2 %copy-start.8 = (f32[2,5,16,20,128]{4,2,3,1,0:T(8,128)S(1)}, f32[2,5,16,20,128]{4,2,3,1,0:T(8,128)}, u32[]{:S(2)}) copy-start(f32[2,5,16,20,128]{4,2,3,1,0:T(8,128)} %copy.83) | copy-start | bytes 4915204
  946.3 107.7 %copy-start.3 = (f32[5,16,16,128]{3,1,2,0:T(8,128)}, f32[5,16,16,128]{3,1,2,0:T(8,128)S(1)}, u32[]{:S(2)}) copy-start(f32[5,16,16,128]{3,1,2,0:T(8,128)S(1)} %copy_add_fusion) | copy-start | bytes 1966084
  946.4 107.7 %collective-permute-start = (f32[5,16,1,128]{3,1,2,0:T(8,128)S(1)}, f32[5,16,1,128]{3,1,2,0:T(8,128)S(1)}, u32[]{:S(2)}, u32[]{:S(2)}) collective-permute-start(f32[5,16,1,128]{3,1,2,0:T(8,128)S(1)} %get-tuple-element.54), channel_id=1, source_target_pairs={{0,4},{4,8},{8,12},{12,16},{16,20},{20,24},{24,28},{1,5},{5,9},{9,... | collective-permute-start | bytes 122888 | tf_op jit(solution)/shard_map/ppermute | solution.py:15
  948.3 105.8 %collective-permute-start.1 = (f32[5,16,1,128]{3,1,2,0:T(8,128)S(1)}, f32[5,16,1,128]{3,1,2,0:T(8,128)S(1)}, u32[]{:S(2)}, u32[]{:S(2)}) collective-permute-start(f32[5,16,1,128]{3,1,2,0:T(8,128)S(1)} %get-tuple-element.55), channel_id=1, source_target_pairs={{4,0},{8,4},{12,8},{16,12},{20,16},{24,20},{28,24},{5,1},{9,5},{13... | collective-permute-start | bytes 122888 | tf_op jit(solution)/shard_map/ppermute | solution.py:18
  1055.0 8.6 collective-permute-start.2
  1058.7 6.4 collective-permute-start.3
  1068.9 1.1 copy-start.5
  1068.9 1.3 copy-start.7
  1069.0 1.3 copy-start.14
  1069.3 1.3 copy-start.4
  1076.3 7.0 collective-permute-start.8
  1078.4 6.3 collective-permute-start.9
  1087.7 6.4 collective-permute-start.10
  1090.2 5.3 collective-permute-start.11
  1099.2 1.1 copy-start.6
  1104.1 2.1 copy-start.1
where the time goes:
time: 1120 us; the launch traced here: 1110 us
  other arithmetic  800 us (71%)
  starting transfers between devices  147 us (13%)
  local copies, waits for them, and re-layouts  123 us (11%)
  waiting for transfers between devices  35.3 us (3%)
    scatter-add x1, other arithmetic, local(): jnp.zeros((3, levels * cols_x * cols_y), jnp.float32).at[:, flat_cells]  760 us
    ppermute x6, starting transfers between devices, with_halo(): lax.ppermute(lax.slice_in_dim(block, 0, width, axis=dim), axis, backward)  121 us
    all_to_all x1, waiting for transfers between devices, local(): lax.all_to_all(values.reshape(devices, capacity, 3, gate_count), ('gx', '...  33.1 us
    reshape x1, local copies, waits for them, and re-layouts, local(): jnp.transpose(got_values.reshape(-1, 3, gate_count), (1, 0, 2))  31.1 us
    slice x1, local copies, waits for them, and re-layouts, local(): forcing[0]  30.5 us
  transfers between devices with their start and end apart: 14, of which 3 were waited for; matrix products, arithmetic and copies ran while one was open for 6% of the time, Pallas kernels for 0%

commit v1 on v0

--- a/solution.py
+++ b/solution.py
@@ -1,6 +1,8 @@
 import jax
 import jax.numpy as jnp
 from jax import lax
+from jax.experimental import pallas as pl
+from jax.experimental.pallas import tpu as pltpu
 from jax.sharding import PartitionSpec as P
 
 diffusion = 0.1
@@ -65,6 +67,85 @@
     return cotangent[..., 2:-2, 2:-2]
 
 
+def scatter_kernel(got, out, acc, lhs, rhs):
+    sources, slots, channels, gates = got.shape
+    rows, cols = out.shape[1:]
+    bf16 = jnp.bfloat16
+    acc[...] = jnp.zeros_like(acc)
+    iota_col = lax.broadcasted_iota(jnp.int32, (cols, gates), 0).astype(jnp.float32).astype(bf16)
+    iota_row = lax.broadcasted_iota(jnp.int32, (rows, gates), 0).astype(jnp.float32).astype(bf16)
+    zero_col = jnp.zeros((cols, gates), bf16)
+    zero_row = jnp.zeros((rows, gates), bf16)
+    one_row = jnp.ones((rows, gates), bf16)
+
+    def one_source(source, carry):
+        for slot in range(slots):
+            span = slice(slot * gates, (slot + 1) * gates)
+            cell = got[source, slot, pl.ds(3, 1), :].astype(jnp.int32)
+            row = (cell // cols).astype(jnp.float32)
+            col = (cell % cols).astype(jnp.float32)
+            row = jnp.broadcast_to(row, (rows, gates)).astype(bf16)
+            col = jnp.broadcast_to(col, (cols, gates)).astype(bf16)
+            hit = iota_col == col
+            for channel in range(3):
+                value = got[source, slot, pl.ds(channel, 1), :]
+                high = value.astype(bf16).astype(jnp.float32)
+                for part, piece in enumerate((high, value - high)):
+                    piece = jnp.broadcast_to(piece, (cols, gates)).astype(bf16)
+                    at = (2 * channel + part) * cols
+                    lhs[at : at + cols, span] = jnp.where(hit, piece, zero_col)
+            rhs[:, span] = jnp.where(iota_row == row, one_row, zero_row)
+        acc[...] += lax.dot_general(
+            lhs[...], rhs[...], (((1,), (1,)), ((), ())), preferred_element_type=jnp.float32
+        )
+        return carry
+
+    lax.fori_loop(0, sources, one_source, 0)
+    for channel in range(3):
+        at = 2 * channel * cols
+        out[channel] = (acc[at : at + cols, :] + acc[at + cols : at + 2 * cols, :]).T
+
+
+def scatter(got, rows, cols):
+    sources, slots, channels, gates = got.shape
+    return pl.pallas_call(
+        scatter_kernel,
+        out_shape=jax.ShapeDtypeStruct((3, rows, cols), jnp.float32),
+        in_specs=[pl.BlockSpec(memory_space=pltpu.VMEM)],
+        out_specs=pl.BlockSpec(memory_space=pltpu.VMEM),
+        scratch_shapes=[
+            pltpu.VMEM((6 * cols, rows), jnp.float32),
+            pltpu.VMEM((6 * cols, slots * gates), jnp.bfloat16),
+            pltpu.VMEM((rows, slots * gates), jnp.bfloat16),
+        ],
+        compiler_params=pltpu.CompilerParams(vmem_limit_bytes=40 * 2**20),
+        name="scatter",
+    )(got)
+
+
+def pack_kernel(from_ray, packed, out):
+    rays = packed.shape[0]
+
+    def one_slot(slot, carry):
+        ray = from_ray[slot]
+        block = packed[jnp.minimum(ray, rays - 1)]
+        out[slot] = jnp.where(ray < rays, block, jnp.zeros_like(block))
+        return carry
+
+    lax.fori_loop(0, out.shape[0], one_slot, 0, unroll=8)
+
+
+def pack(from_ray, packed):
+    return pl.pallas_call(
+        pack_kernel,
+        out_shape=jax.ShapeDtypeStruct(from_ray.shape + packed.shape[1:], jnp.float32),
+        in_specs=[pl.BlockSpec(memory_space=pltpu.SMEM), pl.BlockSpec(memory_space=pltpu.VMEM)],
+        out_specs=pl.BlockSpec(memory_space=pltpu.VMEM),
+        compiler_params=pltpu.CompilerParams(vmem_limit_bytes=16 * 2**20),
+        name="pack",
+    )(from_ray, packed)
+
+
 def local(adjoint_state, trajectory, ray_resid, ray_angle, ray_slope, ray_dest, gate_cell):
     tiles_x = lax.axis_size("gx")
     tiles_y = lax.axis_size("gy")
@@ -87,32 +168,14 @@
     matches = slot_index[None, :] == slot_ids[:, None]
     filled = jnp.any(matches, axis=1)
     source = jnp.sum(jnp.where(matches, positions[None, :], 0), axis=1)
-    values = jnp.take(contrib, source, axis=0) * filled.astype(jnp.float32)[:, None, None]
-    cell_index = jnp.where(filled[:, None], jnp.take(gate_cell, source, axis=0), 0)
-    got_values, got_cells = (
-        lax.all_to_all(
-            values.reshape(devices, capacity, 3, gate_count),
-            ("gx", "gy"),
-            split_axis=0,
-            concat_axis=0,
-            tiled=True,
-        ),
-        lax.all_to_all(
-            cell_index.reshape(devices, capacity, gate_count),
-            ("gx", "gy"),
-            split_axis=0,
-            concat_axis=0,
-            tiled=True,
-        ),
-    )
+    packed = jnp.concatenate([contrib, gate_cell[:, None].astype(jnp.float32)], axis=1)
+    values = pack(jnp.where(filled, source, ray_count), packed)
+    values = values.reshape(devices, capacity, 4, gate_count)
+    got = lax.all_to_all(values, ("gx", "gy"), split_axis=0, concat_axis=0, tiled=True)
     levels = adjoint_state.shape[1]
     cols_x = adjoint_state.shape[2]
     cols_y = adjoint_state.shape[3]
-    flat_values = jnp.transpose(got_values.reshape(-1, 3, gate_count), (1, 0, 2)).reshape(3, -1)
-    flat_cells = got_cells.reshape(-1).astype(jnp.int32)
-    forcing = (
-        jnp.zeros((3, levels * cols_x * cols_y), jnp.float32).at[:, flat_cells].add(flat_values)
-    )
+    forcing = scatter(got, levels * cols_x, cols_y)
     forcing = forcing.reshape(3, levels, cols_x, cols_y)
     blank_field = jnp.zeros_like(forcing[0])
     result = adjoint_state + jnp.stack(

time: 1120 us -> 251 us (0.22); the launches traced: 1110 us -> 250 us
  other arithmetic: 800 us -> 36.7 us
  starting transfers between devices: 147 us -> 38.5 us
  Pallas kernels: 0 us -> 75.9 us
  local copies, waits for them, and re-layouts: 123 us -> 54.1 us
    scatter-add x1 -> x0, other arithmetic: 760 us -> none  [local(): jnp.zeros((3, levels * cols_x * cols_y), jnp.float32).at[:, flat_cells]]
    ppermute x6, starting transfers between devices: 121 us -> 18.3 us  [with_halo(): lax.ppermute(lax.slice_in_dim(block, 0, width, axis=dim), axis, backward)]
    pallas_call x0 -> x2, Pallas kernels: none -> 75.9 us  [the longest x1 72.2 us: scatter(): pl.pallas_call(scatter_kernel, out_shape=jax.ShapeDtypeStruct((3, rows, c...]
    ppermute x6, waiting for transfers between devices: 2.21 us -> 36.5 us  [with_halo(): lax.ppermute(lax.slice_in_dim(block, 0, width, axis=dim), axis, backward)]
    all_to_all x2 -> x1, waiting for transfers between devices: 33.1 us -> 0.01 us  [local(): lax.all_to_all(values, ('gx', 'gy'), split_axis=0, concat_axis=0, tiled=T...]
    reshape x1 -> x0, local copies, waits for them, and re-layouts: 31.1 us -> none  [local(): jnp.transpose(got_values.reshape(-1, 3, gate_count), (1, 0, 2))]
    slice x1, local copies, waits for them, and re-layouts: 30.5 us -> 0.03 us  [local(): forcing[0]]
  transfers between devices with their start and end apart: 14 -> 13, of which waited for: 3 -> 4; matrix products, arithmetic and copies ran while one was open for 6% -> 21% of each run, Pallas kernels for 0% -> 0%
where the time goes in v1:
time: 251 us; the launch traced here: 250 us
  Pallas kernels  75.9 us (30%)
  local copies, waits for them, and re-layouts  54.1 us (22%)
  waiting for transfers between devices  44.5 us (18%)
  starting transfers between devices  38.5 us (15%)
  other arithmetic  36.7 us (15%)
    pallas_call x1, Pallas kernels, scatter(): pl.pallas_call(scatter_kernel, out_shape=jax.ShapeDtypeStruct((3, rows, c...  72.2 us
    ppermute x6, waiting for transfers between devices, with_halo(): lax.ppermute(lax.slice_in_dim(block, 0, width, axis=dim), axis, backward)  36.5 us
    concatenate x6, other arithmetic, with_halo(): block = jnp.concatenate([low, block, high], axis=dim)  19.2 us
    ppermute x6, starting transfers between devices, with_halo(): lax.ppermute(lax.slice_in_dim(block, 0, width, axis=dim), axis, backward)  18.3 us
    unnamed x37, local copies, waits for them, and re-layouts  17.6 us
    ppermute x6, starting transfers between devices, with_halo(): lax.ppermute(lax.slice_in_dim(block, block.shape[dim] - width, None, axis...  14.3 us
    ppermute x4, local copies, waits for them, and re-layouts, with_halo(): lax.ppermute(lax.slice_in_dim(block, block.shape[dim] - width, None, axis...  11.6 us
    ppermute x4, local copies, waits for them, and re-layouts, with_halo(): lax.ppermute(lax.slice_in_dim(block, 0, width, axis=dim), axis, backward)  10.7 us
  transfers between devices with their start and end apart: 13, of which 4 were waited for; matrix products, arithmetic and copies ran while one was open for 21% of the time, Pallas kernels for 0%

profile of v1, /device:TPU:18, one launch (start us, length us, event | category | flops | bytes accessed | tf_op | source)
XLA Modules:
  0.0 250.3 jit_solution(17836085809316912244)
XLA Ops:
  0.0 1.0 convert_reduce_fusion
  3.3 1.7 fusion.50
  5.0 1.0 sine_multiply_fusion
  6.0 1.0 pad_maximum_fusion.4.packed
  7.0 3.8 %pack.1 = f32[1024,4,128]{2,1,0:T(4,128)S(1)} custom-call(s32[1024]{0:T(1024)S(1)} %broadcast_select_fusion.from_ray, f32[512,4,128]{2,1,0:T(4,128)S(1)} %pad_maximum_fusion.4.packed), custom_call_target="tpu_custom_call" | custom-call | tf_op jit(solution)/shard_map/pack/pallas_call | solution.py:139
  10.8 1.3 copy-done
  12.1 5.9 %all-to-all-start = ((f32[32,32,4,128]{3,2,1,0:T(4,128)}), f32[32,32,4,128]{3,2,1,0:T(4,128)S(1)}, u32[]{:S(2)}, u32[]{:S(2)}) async-start(f32[32,32,4,128]{3,2,1,0:T(4,128)} %bitcast.61), calls=%async_computation | async-start | bytes 4194304 | tf_op jit(solution)/shard_map/all_to_all | solution.py:174
  18.9 3.4 %collective-permute-start.5 = (f32[2,5,16,2,128]{4,2,3,1,0:T(8,128)}, f32[2,5,16,2,128]{4,2,3,1,0:T(8,128)}, u32[]{:S(2)}, u32[]{:S(2)}) collective-permute-start(f32[2,5,16,2,128]{4,2,3,1,0:T(8,128)} %copy.70), channel_id=1, source_target_pairs={{4,0},{8,4},{12,8},{16,12},{20,16},{24,20},{28,24},{5,1},{9,5},{13... | collective-permute-start | bytes 491528 | tf_op jit(solution)/shard_map/ppermute | solution.py:20
  22.9 2.5 collective-permute-start.4
  25.4 5.5 %copy.55 = f32[2,5,16,16,128]{3,2,4,1,0:T(8,128)} copy(f32[2,5,16,16,128]{4,3,2,1,0:T(8,128)S(1)} %copy-done.10) | data formatting | bytes 2621440 | tf_op args[1]
  30.9 36.5 %collective-permute-done.5 = f32[2,5,16,2,128]{4,2,3,1,0:T(8,128)} collective-permute-done((f32[2,5,16,2,128]{4,2,3,1,0:T(8,128)}, f32[2,5,16,2,128]{4,2,3,1,0:T(8,128)}, u32[]{:S(2)}, u32[]{:S(2)}) %collective-permute-start.5) | collective-permute-done | bytes 163872 | tf_op jit(solution)/shard_map/ppermute | solution.py:20
  67.3 6.3 %copy.56 = f32[2,5,16,2,128]{3,2,4,1,0:T(8,128)} copy(f32[2,5,16,2,128]{4,2,3,1,0:T(8,128)} %collective-permute-done.5) | data formatting | bytes 327680 | tf_op jit(solution)/shard_map/ppermute | solution.py:20
  73.6 6.4 %copy.54 = f32[2,5,16,2,128]{3,2,4,1,0:T(8,128)} copy(f32[2,5,16,2,128]{4,2,3,1,0:T(8,128)} %collective-permute-done.4) | data formatting | bytes 327680 | tf_op jit(solution)/shard_map/ppermute | solution.py:17
  80.0 12.2 %pad_maximum_fusion = f32[2,5,16,20,128]{3,2,4,1,0:T(8,128)S(1)} fusion(f32[2,5,16,2,128]{3,2,4,1,0:T(8,128)} %copy.56, f32[2,5,16,16,128]{3,2,4,1,0:T(8,128)} %copy.55, f32[2,5,16,2,128]{3,2,4,1,0:T(8,128)} %copy.54), kind=kLoop, calls=%fused_computation | loop fusion | flops 819200 | bytes 3276800 | tf_op jit(solution)/shard_map/concatenate | solution.py:21
  92.2 4.0 %copy-done.1 = f32[2,5,16,20,128]{3,2,4,1,0:T(8,128)} copy-done((f32[2,5,16,20,128]{3,2,4,1,0:T(8,128)}, f32[2,5,16,20,128]{3,2,4,1,0:T(8,128)S(1)}, u32[]{:S(2)}) %copy-start.1) | copy-done | bytes 1638424
  96.2 1.9 collective-permute-start.7
  98.1 2.6 %collective-permute-start.6 = (f32[2,5,16,20,2]{3,2,4,1,0:T(8,128)S(1)}, f32[2,5,16,20,2]{3,2,4,1,0:T(8,128)S(1)}, u32[]{:S(2)}, u32[]{:S(2)}) collective-permute-start(f32[2,5,16,20,2]{3,2,4,1,0:T(8,128)S(1)} %get-tuple-element.21), channel_id=1, source_target_pairs={{0,1},{1,2},{2,3},{4,5},{5,6},{6,7},{8,9},{9,10},{10,11},{12,13},{... | collective-permute-start | bytes 76808 | tf_op jit(solution)/shard_map/ppermute | solution.py:17
  100.8 7.0 %copy.58 = f32[2,5,16,20,128]{4,2,3,1,0:T(8,128)} copy(f32[2,5,16,20,128]{3,2,4,1,0:T(8,128)} %copy-done.1) | data formatting | bytes 3276800 | tf_op jit(solution)/shard_map/concatenate | solution.py:21
  107.9 2.4 copy.59
  110.2 2.3 copy.57
  112.5 72.2 %scatter.1 = f32[3,256,128]{2,1,0:T(8,128)S(1)} custom-call(f32[32,32,4,128]{3,2,1,0:T(4,128)S(1)} %all-to-all-done.got), custom_call_target="tpu_custom_call" | custom-call | tf_op jit(solution)/shard_map/scatter/pallas_call | solution.py:111
  185.3 5.4 %collective-permute-start.1 = (f32[5,16,1,128]{3,1,2,0:T(8,128)S(1)}, f32[5,16,1,128]{3,1,2,0:T(8,128)S(1)}, u32[]{:S(2)}, u32[]{:S(2)}) collective-permute-start(f32[5,16,1,128]{3,1,2,0:T(8,128)S(1)} %get-tuple-element.52), channel_id=1, source_target_pairs={{4,0},{8,4},{12,8},{16,12},{20,16},{24,20},{28,24},{5,1},{9,5},{13... | collective-permute-start | bytes 122888 | tf_op jit(solution)/shard_map/ppermute | solution.py:20
  190.7 1.9 collective-permute-start
  192.7 3.0 %pad_maximum_fusion.1 = f32[2,5,16,20,132]{4,2,3,1,0:T(8,128)} fusion(f32[2,5,16,20,2]{4,2,3,1,0:T(8,128)S(1)} %copy-done.7, f32[2,5,16,20,128]{4,2,3,1,0:T(8,128)S(1)} %copy-done.9, f32[2,5,16,20,2]{4,2,3,1,0:T(8,128)S(1)} %copy-done.8), kind=kLoop, calls=%fused_computation.1 | loop fusion | flops 844800 | bytes 3379200 | tf_op jit(solution)/shard_map/concatenate | solution.py:21
  195.7 1.8 collective-permute-done
  198.5 2.2 collective-permute-start.3
  201.2 2.3 collective-permute-start.2
  203.6 2.5 slice_bitcast_fusion.1
  206.1 1.5 copy.51
  207.5 1.5 copy.50
  209.0 2.2 pad_maximum_fusion.2
  213.6 1.2 fusion.12
  214.8 1.0 fusion.42
  215.9 2.7 %pad_add_fusion.1 = f32[5,16,20,132]{3,1,2,0:T(8,128)S(1)} fusion(f32[5,16,18,130]{3,1,2,0:T(8,128)S(1)} %get-tuple-element.44, f32[5,16,18,130]{3,1,2,0:T(8,128)S(1)} %get-tuple-element.43, f32[5,16,18,130]{3,1,2,0:T(8,128)S(1)} %get-tuple-element.42, f32[5,16,18,130]{3,1,2,0:T(8,128)S(1)} %get-tuple-element.18, ...), kind=kLoop, calls=%fused_computation.8 | loop fusion | flops 1689600 | bytes 5337600 | tf_op jit(solution)/shard_map/transpose(jvp())/add_any | solution.py:26
  218.7 3.2 %collective-permute-start.9 = (f32[5,16,1,128]{3,1,2,0:T(8,128)S(1)}, f32[5,16,1,128]{3,1,2,0:T(8,128)S(1)}, u32[]{:S(2)}, u32[]{:S(2)}) collective-permute-start(f32[5,16,1,128]{3,1,2,0:T(8,128)S(1)} %get-tuple-element.29), channel_id=1, source_target_pairs={{4,0},{8,4},{12,8},{16,12},{20,16},{24,20},{28,24},{5,1},{9,5},{13... | collective-permute-start | bytes 122888 | tf_op jit(solution)/shard_map/ppermute | solution.py:20
  221.9 2.7 %collective-permute-start.8 = (f32[5,16,1,128]{3,1,2,0:T(8,128)S(1)}, f32[5,16,1,128]{3,1,2,0:T(8,128)S(1)}, u32[]{:S(2)}, u32[]{:S(2)}) collective-permute-start(f32[5,16,1,128]{3,1,2,0:T(8,128)S(1)} %get-tuple-element.28), channel_id=1, source_target_pairs={{0,4},{4,8},{8,12},{12,16},{16,20},{20,24},{24,28},{1,5},{5,9},{9,... | collective-permute-start | bytes 122888 | tf_op jit(solution)/shard_map/ppermute | solution.py:17
  224.8 3.9 %collective-permute-done.8 = f32[5,16,1,128]{3,1,2,0:T(8,128)S(1)} collective-permute-done((f32[5,16,1,128]{3,1,2,0:T(8,128)S(1)}, f32[5,16,1,128]{3,1,2,0:T(8,128)S(1)}, u32[]{:S(2)}, u32[]{:S(2)}) %collective-permute-start.8) | collective-permute-done | bytes 40992 | tf_op jit(solution)/shard_map/ppermute | solution.py:17
  228.8 1.1 fusion.47
  229.9 1.7 copy.72
  231.5 2.2 collective-permute-start.11
  234.3 2.3 collective-permute-start.10
  237.3 2.3 collective-permute-done.10
  239.7 1.5 copy.62
  241.1 1.8 pad_maximum_fusion.3
  245.0 1.2 fusion.6
  247.1 1.1 fusion.40
  248.2 1.1 pad_add_fusion.4
  249.3 1.0 copy.64
  (71 shorter events, 12.8 us)
Async XLA Ops:
  0.0 4.9 %copy-start.12 = (f32[512,128]{1,0:T(8,128)S(1)}, f32[512,128]{1,0:T(8,128)}, u32[]{:S(2)}) copy-start(f32[512,128]{1,0:T(8,128)} %param.11) | copy-start | bytes 786436
  0.0 5.0 %copy-start.13 = (f32[512,128]{1,0:T(8,128)S(1)}, f32[512,128]{1,0:T(8,128)}, u32[]{:S(2)}) copy-start(f32[512,128]{1,0:T(8,128)} %param.10) | copy-start | bytes 786436
  10.8 1.3 copy-start
  12.1 5.9 %copy-start.10 = (f32[2,5,16,16,128]{4,3,2,1,0:T(8,128)S(1)}, f32[2,5,16,16,128]{4,3,2,1,0:T(8,128)}, u32[]{:S(2)}) copy-start(f32[2,5,16,16,128]{4,3,2,1,0:T(8,128)} %param.8) | copy-start | bytes 3932164
  12.1 100.5 %all-to-all-start = ((f32[32,32,4,128]{3,2,1,0:T(4,128)}), f32[32,32,4,128]{3,2,1,0:T(4,128)S(1)}, u32[]{:S(2)}, u32[]{:S(2)}) async-start(f32[32,32,4,128]{3,2,1,0:T(4,128)} %bitcast.61), calls=%async_computation | async-start | bytes 4194304 | tf_op jit(solution)/shard_map/all_to_all | solution.py:174
  18.9 48.5 %collective-permute-start.5 = (f32[2,5,16,2,128]{4,2,3,1,0:T(8,128)}, f32[2,5,16,2,128]{4,2,3,1,0:T(8,128)}, u32[]{:S(2)}, u32[]{:S(2)}) collective-permute-start(f32[2,5,16,2,128]{4,2,3,1,0:T(8,128)} %copy.70), channel_id=1, source_target_pairs={{4,0},{8,4},{12,8},{16,12},{20,16},{24,20},{28,24},{5,1},{9,5},{13... | collective-permute-start | bytes 491528 | tf_op jit(solution)/shard_map/ppermute | solution.py:20
  22.9 50.7 %collective-permute-start.4 = (f32[2,5,16,2,128]{4,2,3,1,0:T(8,128)}, f32[2,5,16,2,128]{4,2,3,1,0:T(8,128)}, u32[]{:S(2)}, u32[]{:S(2)}) collective-permute-start(f32[2,5,16,2,128]{4,2,3,1,0:T(8,128)} %copy.69), channel_id=1, source_target_pairs={{0,4},{4,8},{8,12},{12,16},{16,20},{20,24},{24,28},{1,5},{5,9},{9,... | collective-permute-start | bytes 491528 | tf_op jit(solution)/shard_map/ppermute | solution.py:17
  92.2 4.0 %copy-start.1 = (f32[2,5,16,20,128]{3,2,4,1,0:T(8,128)}, f32[2,5,16,20,128]{3,2,4,1,0:T(8,128)S(1)}, u32[]{:S(2)}) copy-start(f32[2,5,16,20,128]{3,2,4,1,0:T(8,128)S(1)} %pad_maximum_fusion) | copy-start | bytes 4915204
  96.2 11.7 %collective-permute-start.7 = (f32[2,5,16,20,2]{3,2,4,1,0:T(8,128)S(1)}, f32[2,5,16,20,2]{3,2,4,1,0:T(8,128)S(1)}, u32[]{:S(2)}, u32[]{:S(2)}) collective-permute-start(f32[2,5,16,20,2]{3,2,4,1,0:T(8,128)S(1)} %get-tuple-element.22), channel_id=1, source_target_pairs={{1,0},{2,1},{3,2},{5,4},{6,5},{7,6},{9,8},{10,9},{11,10},{13,12},{... | collective-permute-start | bytes 76808 | tf_op jit(solution)/shard_map/ppermute | solution.py:20
  98.1 12.1 %collective-permute-start.6 = (f32[2,5,16,20,2]{3,2,4,1,0:T(8,128)S(1)}, f32[2,5,16,20,2]{3,2,4,1,0:T(8,128)S(1)}, u32[]{:S(2)}, u32[]{:S(2)}) collective-permute-start(f32[2,5,16,20,2]{3,2,4,1,0:T(8,128)S(1)} %get-tuple-element.21), channel_id=1, source_target_pairs={{0,1},{1,2},{2,3},{4,5},{5,6},{6,7},{8,9},{9,10},{10,11},{12,13},{... | collective-permute-start | bytes 76808 | tf_op jit(solution)/shard_map/ppermute | solution.py:17
  112.5 72.3 %copy-start.11 = (f32[5,16,16,128]{3,2,1,0:T(8,128)S(1)}, f32[5,16,16,128]{3,2,1,0:T(8,128)}, u32[]{:S(2)}) copy-start(f32[5,16,16,128]{3,2,1,0:T(8,128)} %param.7) | copy-start | bytes 1966084
  112.5 80.1 %copy-start.9 = (f32[2,5,16,20,128]{4,2,3,1,0:T(8,128)S(1)}, f32[2,5,16,20,128]{4,2,3,1,0:T(8,128)}, u32[]{:S(2)}) copy-start(f32[2,5,16,20,128]{4,2,3,1,0:T(8,128)} %copy.58) | copy-start | bytes 4915204
  184.7 8.0 %copy-start.8 = (f32[2,5,16,20,2]{4,2,3,1,0:T(8,128)S(1)}, f32[2,5,16,20,2]{4,2,3,1,0:T(8,128)}, u32[]{:S(2)}) copy-start(f32[2,5,16,20,2]{4,2,3,1,0:T(8,128)} %copy.57) | copy-start | bytes 76804
  184.8 7.9 %copy-start.7 = (f32[2,5,16,20,2]{4,2,3,1,0:T(8,128)S(1)}, f32[2,5,16,20,2]{4,2,3,1,0:T(8,128)}, u32[]{:S(2)}) copy-start(f32[2,5,16,20,2]{4,2,3,1,0:T(8,128)} %copy.59) | copy-start | bytes 76804
  185.3 12.2 %copy-start.2 = (f32[5,16,16,128]{3,1,2,0:T(8,128)}, f32[5,16,16,128]{3,1,2,0:T(8,128)S(1)}, u32[]{:S(2)}) copy-start(f32[5,16,16,128]{3,1,2,0:T(8,128)S(1)} %copy_add_fusion) | copy-start | bytes 1966084
  185.3 10.4 %collective-permute-start.1 = (f32[5,16,1,128]{3,1,2,0:T(8,128)S(1)}, f32[5,16,1,128]{3,1,2,0:T(8,128)S(1)}, u32[]{:S(2)}, u32[]{:S(2)}) collective-permute-start(f32[5,16,1,128]{3,1,2,0:T(8,128)S(1)} %get-tuple-element.52), channel_id=1, source_target_pairs={{4,0},{8,4},{12,8},{16,12},{20,16},{24,20},{28,24},{5,1},{9,5},{13... | collective-permute-start | bytes 122888 | tf_op jit(solution)/shard_map/ppermute | solution.py:20
  190.7 6.8 %collective-permute-start = (f32[5,16,1,128]{3,1,2,0:T(8,128)S(1)}, f32[5,16,1,128]{3,1,2,0:T(8,128)S(1)}, u32[]{:S(2)}, u32[]{:S(2)}) collective-permute-start(f32[5,16,1,128]{3,1,2,0:T(8,128)S(1)} %get-tuple-element.51), channel_id=1, source_target_pairs={{0,4},{4,8},{8,12},{12,16},{16,20},{20,24},{24,28},{1,5},{5,9},{9,... | collective-permute-start | bytes 122888 | tf_op jit(solution)/shard_map/ppermute | solution.py:17
  198.5 7.6 %collective-permute-start.3 = (f32[5,16,18,1]{2,1,3,0:T(8,128)S(1)}, f32[5,16,18,1]{2,1,3,0:T(8,128)S(1)}, u32[]{:S(2)}, u32[]{:S(2)}) collective-permute-start(f32[5,16,18,1]{2,1,3,0:T(8,128)S(1)} %copy.68), channel_id=1, source_target_pairs={{1,0},{2,1},{3,2},{5,4},{6,5},{7,6},{9,8},{10,9},{11,10},{13,12},{... | collective-permute-start | bytes 17288 | tf_op jit(solution)/shard_map/ppermute | solution.py:20
  201.2 6.3 %collective-permute-start.2 = (f32[5,16,18,1]{2,1,3,0:T(8,128)S(1)}, f32[5,16,18,1]{2,1,3,0:T(8,128)S(1)}, u32[]{:S(2)}, u32[]{:S(2)}) collective-permute-start(f32[5,16,18,1]{2,1,3,0:T(8,128)S(1)} %copy.67), channel_id=1, source_target_pairs={{0,1},{1,2},{2,3},{4,5},{5,6},{6,7},{8,9},{9,10},{10,11},{12,13},{... | collective-permute-start | bytes 17288 | tf_op jit(solution)/shard_map/ppermute | solution.py:17
  211.2 1.1 copy-start.6
  211.5 1.1 copy-start.3
  211.6 1.4 copy-start.4
  211.6 1.4 copy-start.14
  218.7 6.1 %collective-permute-start.9 = (f32[5,16,1,128]{3,1,2,0:T(8,128)S(1)}, f32[5,16,1,128]{3,1,2,0:T(8,128)S(1)}, u32[]{:S(2)}, u32[]{:S(2)}) collective-permute-start(f32[5,16,1,128]{3,1,2,0:T(8,128)S(1)} %get-tuple-element.29), channel_id=1, source_target_pairs={{4,0},{8,4},{12,8},{16,12},{20,16},{24,20},{28,24},{5,1},{9,5},{13... | collective-permute-start | bytes 122888 | tf_op jit(solution)/shard_map/ppermute | solution.py:20
  221.9 6.8 %collective-permute-start.8 = (f32[5,16,1,128]{3,1,2,0:T(8,128)S(1)}, f32[5,16,1,128]{3,1,2,0:T(8,128)S(1)}, u32[]{:S(2)}, u32[]{:S(2)}) collective-permute-start(f32[5,16,1,128]{3,1,2,0:T(8,128)S(1)} %get-tuple-element.28), channel_id=1, source_target_pairs={{0,4},{4,8},{8,12},{12,16},{16,20},{20,24},{24,28},{1,5},{5,9},{9,... | collective-permute-start | bytes 122888 | tf_op jit(solution)/shard_map/ppermute | solution.py:17
  231.5 5.2 %collective-permute-start.11 = (f32[5,16,18,1]{2,1,3,0:T(8,128)S(1)}, f32[5,16,18,1]{2,1,3,0:T(8,128)S(1)}, u32[]{:S(2)}, u32[]{:S(2)}) collective-permute-start(f32[5,16,18,1]{2,1,3,0:T(8,128)S(1)} %copy.72), channel_id=1, source_target_pairs={{1,0},{2,1},{3,2},{5,4},{6,5},{7,6},{9,8},{10,9},{11,10},{13,12},{... | collective-permute-start | bytes 17288 | tf_op jit(solution)/shard_map/ppermute | solution.py:20
  234.3 5.3 %collective-permute-start.10 = (f32[5,16,18,1]{2,1,3,0:T(8,128)S(1)}, f32[5,16,18,1]{2,1,3,0:T(8,128)S(1)}, u32[]{:S(2)}, u32[]{:S(2)}) collective-permute-start(f32[5,16,18,1]{2,1,3,0:T(8,128)S(1)} %copy.71), channel_id=1, source_target_pairs={{0,1},{1,2},{2,3},{4,5},{5,6},{6,7},{8,9},{9,10},{10,11},{12,13},{... | collective-permute-start | bytes 17288 | tf_op jit(solution)/shard_map/ppermute | solution.py:17
  243.2 1.1 copy-start.5

commit v2 on v1

--- a/solution.py
+++ b/solution.py
@@ -9,62 +9,41 @@
 latent = 2.0
 
 
-def with_halo(block, sides, width):
-    for axis, dim in sides:
-        count = lax.axis_size(axis)
-        forward = [(i, i + 1) for i in range(count - 1)]
-        backward = [(target, source) for source, target in forward]
-        low = lax.ppermute(
-            lax.slice_in_dim(block, block.shape[dim] - width, None, axis=dim), axis, forward
-        )
-        high = lax.ppermute(lax.slice_in_dim(block, 0, width, axis=dim), axis, backward)
-        block = jnp.concatenate([low, block, high], axis=dim)
-    return block
+def from_next(edge, axis):
+    count = lax.axis_size(axis)
+    return lax.ppermute(edge, axis, [(i + 1, i) for i in range(count - 1)])
 
 
-def f_valid(state_pad, traj_pad):
-    center = state_pad[..., 1:-1, 1:-1]
-    diff_x = 0.5 * (state_pad[..., 2:, 1:-1] - state_pad[..., :-2, 1:-1])
-    diff_y = 0.5 * (state_pad[..., 1:-1, 2:] - state_pad[..., 1:-1, :-2])
-    laplace = (
-        state_pad[..., 2:, 1:-1]
-        + state_pad[..., :-2, 1:-1]
-        + state_pad[..., 1:-1, 2:]
-        + state_pad[..., 1:-1, :-2]
-        - 4.0 * center
-    )
-    grad_x = 0.5 * (traj_pad[..., 2:, 1:-1] - traj_pad[..., :-2, 1:-1])
-    grad_y = 0.5 * (traj_pad[..., 1:-1, 2:] - traj_pad[..., 1:-1, :-2])
-    wind_u = traj_pad[0, :, 1:-1, 1:-1]
-    wind_v = traj_pad[1, :, 1:-1, 1:-1]
-    advected = (
-        center
-        - (wind_u * diff_x + wind_v * diff_y)
-        - (center[0] * grad_x + center[1] * grad_y)
-        + diffusion * laplace
-    )
-    convert = 0.3 * jax.nn.sigmoid(traj_pad[2, :, 1:-1, 1:-1])
-    falling = 0.3 * jax.nn.sigmoid(traj_pad[4, :, 1:-1, 1:-1])
-    condensed = convert * advected[3]
-    rain_old = advected[4]
-    from_above = jnp.concatenate([rain_old[1:], jnp.zeros_like(rain_old[:1])], axis=0)
-    rain_new = rain_old + condensed + falling * (from_above - rain_old)
-    return jnp.stack(
-        [
-            advected[0],
-            advected[1],
-            advected[2] + latent * condensed,
-            advected[3] - condensed,
-            rain_new,
-        ]
-    )
+def from_previous(edge, axis):
+    count = lax.axis_size(axis)
+    return lax.ppermute(edge, axis, [(i, i + 1) for i in range(count - 1)])
 
 
-def adjoint_region(cot_ext, traj_ext):
-    primal = jnp.zeros_like(traj_ext)
-    unused, pullback = jax.vjp(lambda state_pad: f_valid(state_pad, traj_ext), primal)
-    cotangent = pullback(cot_ext)[0]
-    return cotangent[..., 2:-2, 2:-2]
+def shifted(above, below, axis, dim):
+    size = above.shape[dim]
+    last = from_next(lax.slice_in_dim(above, 0, 1, axis=dim), axis)
+    first = from_previous(lax.slice_in_dim(below, size - 1, size, axis=dim), axis)
+    up = jnp.concatenate([lax.slice_in_dim(above, 1, size, axis=dim), last], axis=dim)
+    down = jnp.concatenate([first, lax.slice_in_dim(below, 0, size - 1, axis=dim)], axis=dim)
+    return up, down
+
+
+def adjoint_step(cot, traj, slope_x, slope_y):
+    convert = 0.3 * jax.nn.sigmoid(traj[2])
+    falling = 0.3 * jax.nn.sigmoid(traj[4])
+    condensed = convert * (latent * cot[2] - cot[3] + cot[4])
+    fallen = falling * cot[4]
+    into_below = jnp.concatenate([jnp.zeros_like(fallen[:1]), fallen[:-1]], axis=0)
+    own = jnp.stack([cot[0], cot[1], cot[2], cot[3] + condensed, cot[4] - fallen + into_below])
+    half_u, half_v = 0.5 * traj[0], 0.5 * traj[1]
+    up_x, down_x = shifted((diffusion + half_u) * own, (diffusion - half_u) * own, "gx", 2)
+    up_y, down_y = shifted((diffusion + half_v) * own, (diffusion - half_v) * own, "gy", 3)
+    result = (1.0 - 4.0 * diffusion) * own + up_x + down_x + up_y + down_y
+    blank = jnp.zeros_like(traj[0])
+    wind = jnp.stack(
+        [jnp.sum(own * slope_x, axis=0), jnp.sum(own * slope_y, axis=0), blank, blank, blank]
+    )
+    return result - wind
 
 
 def scatter_kernel(got, out, acc, lhs, rhs):
@@ -181,11 +160,11 @@
     result = adjoint_state + jnp.stack(
         [forcing[0], forcing[1], blank_field, blank_field, forcing[2]]
     )
-    rim_width = 2
-    traj_ext = with_halo(trajectory, (("gx", 3), ("gy", 4)), rim_width)
+    next_x, last_x = shifted(trajectory, trajectory, "gx", 3)
+    next_y, last_y = shifted(trajectory, trajectory, "gy", 4)
+    slope_x, slope_y = 0.5 * (next_x - last_x), 0.5 * (next_y - last_y)
     for section in (1, 0):
-        extended = with_halo(result, (("gx", 2), ("gy", 3)), 1)
-        result = adjoint_region(extended, traj_ext[section])
+        result = adjoint_step(result, trajectory[section], slope_x[section], slope_y[section])
     return result
 
 

time: 251 us -> 208 us (0.83); the launches traced: 250 us -> 204 us
  waiting for transfers between devices: 44.5 us -> 14.2 us
  other arithmetic: 36.7 us -> 20.9 us
    ppermute x12, waiting for transfers between devices: 44.5 us -> 14.2 us  [the longest x6 11.8 us: from_next(): return lax.ppermute(edge, axis, [(i + 1, i) for i in range(count - 1)])]
    concatenate x6 -> x0, other arithmetic: 19.2 us -> none  [with_halo(): block = jnp.concatenate([low, block, high], axis=dim)]
    slice x8 -> x28, local copies, waits for them, and re-layouts: 2.9 us -> 21.1 us  [the longest x8 8.63 us: shifted(): lax.slice_in_dim(below, size - 1, size, axis=dim)]
    ppermute x8 -> x6, local copies, waits for them, and re-layouts: 22.3 us -> 14.6 us  [the longest x3 7.32 us: from_next(): return lax.ppermute(edge, axis, [(i + 1, i) for i in range(count - 1)])]
    concatenate x1 -> x0, local copies, waits for them, and re-layouts: 7.04 us -> none  [with_halo(): block = jnp.concatenate([low, block, high], axis=dim)]
    unnamed x37 -> x52, local copies, waits for them, and re-layouts: 17.6 us -> 10.7 us
    sub x0 -> x3, other arithmetic: none -> 6.07 us  [the longest x2 5.19 us: adjoint_step(): return result - wind]
    mul x6, other arithmetic: 2.35 us -> 7.44 us  [the longest x2 6.87 us: local(): slope_x, slope_y = (0.5 * (next_x - last_x), 0.5 * (next_y - last_y))]
  transfers between devices with their start and end apart: 13 -> 13, of which waited for: 4 -> 2; matrix products, arithmetic and copies ran while one was open for 21% -> 26% of each run, Pallas kernels for 0% -> 0%
where the time goes in v2:
time: 208 us; the launch traced here: 204 us
  Pallas kernels  75.9 us (36%)
  local copies, waits for them, and re-layouts  52.8 us (25%)
  starting transfers between devices  39.8 us (19%)
  other arithmetic  20.9 us (10%)
  waiting for transfers between devices  14.2 us (7%)
    pallas_call x1, Pallas kernels, scatter(): pl.pallas_call(scatter_kernel, out_shape=jax.ShapeDtypeStruct((3, rows, c...  72.2 us
    ppermute x6, starting transfers between devices, from_next(): return lax.ppermute(edge, axis, [(i + 1, i) for i in range(count - 1)])  19.9 us
    ppermute x6, starting transfers between devices, from_previous(): return lax.ppermute(edge, axis, [(i, i + 1) for i in range(count - 1)])  14 us
    ppermute x6, waiting for transfers between devices, from_next(): return lax.ppermute(edge, axis, [(i + 1, i) for i in range(count - 1)])  11.8 us
    unnamed x52, local copies, waits for them, and re-layouts  10.7 us
    slice x8, local copies, waits for them, and re-layouts, shifted(): lax.slice_in_dim(below, size - 1, size, axis=dim)  8.63 us
    ppermute x3, local copies, waits for them, and re-layouts, from_next(): return lax.ppermute(edge, axis, [(i + 1, i) for i in range(count - 1)])  7.32 us
    ppermute x3, local copies, waits for them, and re-layouts, from_previous(): return lax.ppermute(edge, axis, [(i, i + 1) for i in range(count - 1)])  7.31 us
  transfers between devices with their start and end apart: 13, of which 2 were waited for; matrix products, arithmetic and copies ran while one was open for 26% of the time, Pallas kernels for 0%

profile of v2, /device:TPU:18, one launch (start us, length us, event | category | flops | bytes accessed | tf_op | source)
XLA Modules:
  0.0 204.2 jit_solution(15828683147986060759)
XLA Ops:
  0.0 1.0 convert_reduce_fusion
  2.3 1.7 fusion.36
  6.0 1.0 pad_maximum_fusion.packed
  7.0 3.8 %pack.1 = f32[1024,4,128]{2,1,0:T(4,128)S(1)} custom-call(s32[1024]{0:T(1024)S(1)} %broadcast_select_fusion.from_ray, f32[512,4,128]{2,1,0:T(4,128)S(1)} %pad_maximum_fusion.packed), custom_call_target="tpu_custom_call" | custom-call | tf_op jit(solution)/shard_map/pack/pallas_call | solution.py:118
  10.8 1.3 copy-done
  12.2 5.9 %all-to-all-start = ((f32[32,32,4,128]{3,2,1,0:T(4,128)}), f32[32,32,4,128]{3,2,1,0:T(4,128)S(1)}, u32[]{:S(2)}, u32[]{:S(2)}) async-start(f32[32,32,4,128]{3,2,1,0:T(4,128)} %bitcast.100), calls=%async_computation | async-start | bytes 4194304 | tf_op jit(solution)/shard_map/all_to_all | solution.py:153
  18.1 1.9 fusion.32
  20.0 3.0 %copy.164 = f32[2,5,16,16,1]{3,2,4,1,0:T(8,128)} copy(f32[2,5,16,16,1]{4,3,2,1,0:T(8,128)} %get-tuple-element.18) | data formatting | bytes 20480
  23.0 2.2 %collective-permute-start.6 = (f32[2,5,16,16,1]{3,2,4,1,0:T(8,128)}, f32[2,5,16,16,1]{3,2,4,1,0:T(8,128)}, u32[]{:S(2)}, u32[]{:S(2)}) collective-permute-start(f32[2,5,16,16,1]{3,2,4,1,0:T(8,128)} %copy.164), channel_id=1, source_target_pairs={{1,0},{2,1},{3,2},{5,4},{6,5},{7,6},{9,8},{10,9},{11,10},{13,12},{... | collective-permute-start | bytes 30728 | tf_op jit(solution)/shard_map/ppermute | solution.py:14
  25.2 2.9 %copy.165 = f32[2,5,16,16,1]{3,2,4,1,0:T(8,128)} copy(f32[2,5,16,16,1]{4,3,2,1,0:T(8,128)} %get-tuple-element.17) | data formatting | bytes 20480
  28.1 2.7 %collective-permute-start.7 = (f32[2,5,16,16,1]{3,2,4,1,0:T(8,128)}, f32[2,5,16,16,1]{3,2,4,1,0:T(8,128)}, u32[]{:S(2)}, u32[]{:S(2)}) collective-permute-start(f32[2,5,16,16,1]{3,2,4,1,0:T(8,128)} %copy.165), channel_id=1, source_target_pairs={{0,1},{1,2},{2,3},{4,5},{5,6},{6,7},{8,9},{9,10},{10,11},{12,13},{... | collective-permute-start | bytes 30728 | tf_op jit(solution)/shard_map/ppermute | solution.py:19
  31.6 3.4 %collective-permute-start.4 = (f32[2,5,16,1,128]{4,2,3,1,0:T(8,128)}, f32[2,5,16,1,128]{4,2,3,1,0:T(8,128)}, u32[]{:S(2)}, u32[]{:S(2)}) collective-permute-start(f32[2,5,16,1,128]{4,2,3,1,0:T(8,128)} %bitcast.47), channel_id=1, source_target_pairs={{4,0},{8,4},{12,8},{16,12},{20,16},{24,20},{28,24},{5,1},{9,5},{13... | collective-permute-start | bytes 245768 | tf_op jit(solution)/shard_map/ppermute | solution.py:14
  35.0 2.5 %collective-permute-start.5 = (f32[2,5,16,1,128]{4,2,3,1,0:T(8,128)S(1)}, f32[2,5,16,1,128]{4,2,3,1,0:T(8,128)}, u32[]{:S(2)}, u32[]{:S(2)}) collective-permute-start(f32[2,5,16,1,128]{4,2,3,1,0:T(8,128)S(1)} %bitcast.118), channel_id=1, source_target_pairs={{0,4},{4,8},{8,12},{12,16},{16,20},{20,24},{24,28},{1,5},{5,9},{9,... | collective-permute-start | bytes 245768 | tf_op jit(solution)/shard_map/ppermute | solution.py:19
  37.4 2.0 fusion.33
  39.4 1.8 fusion.35
  43.5 3.0 %copy.145 = f32[2,5,16,16,1]{4,3,2,1,0:T(8,128)} copy(f32[2,5,16,16,1]{3,2,4,1,0:T(8,128)} %collective-permute-done.6) | data formatting | bytes 20480 | tf_op jit(solution)/shard_map/ppermute | solution.py:14
  46.4 2.9 %copy.147 = f32[2,5,16,16,1]{4,3,2,1,0:T(8,128)} copy(f32[2,5,16,16,1]{3,2,4,1,0:T(8,128)} %collective-permute-done.7) | data formatting | bytes 20480 | tf_op jit(solution)/shard_map/ppermute | solution.py:19
  49.4 4.5 %fusion.2 = f32[2,5,16,16,128]{4,3,2,1,0:T(8,128)} fusion(f32[2,5,16,16,1]{4,3,2,1,0:T(8,128)} %copy.145, f32[2,5,16,16,127]{4,3,2,1,0:T(8,128)} %get-tuple-element.20, f32[2,5,16,16,127]{4,3,2,1,0:T(8,128)} %get-tuple-element.19, f32[2,5,16,16,1]{4,3,2,1,0:T(8,128)} %copy.147), kind=kLoop, calls=%fused_computation.6 | loop fusion | flops 1310720 | bytes 3932160 | tf_op jit(solution)/shard_map/mul | solution.py:165
  53.9 11.8 %collective-permute-done.4 = f32[2,5,16,1,128]{4,2,3,1,0:T(8,128)} collective-permute-done((f32[2,5,16,1,128]{4,2,3,1,0:T(8,128)}, f32[2,5,16,1,128]{4,2,3,1,0:T(8,128)}, u32[]{:S(2)}, u32[]{:S(2)}) %collective-permute-start.4) | collective-permute-done | bytes 81952 | tf_op jit(solution)/shard_map/ppermute | solution.py:14
  65.7 2.3 %collective-permute-done.5 = f32[2,5,16,1,128]{4,2,3,1,0:T(8,128)} collective-permute-done((f32[2,5,16,1,128]{4,2,3,1,0:T(8,128)S(1)}, f32[2,5,16,1,128]{4,2,3,1,0:T(8,128)}, u32[]{:S(2)}, u32[]{:S(2)}) %collective-permute-start.5) | collective-permute-done | bytes 81952 | tf_op jit(solution)/shard_map/ppermute | solution.py:19
  68.0 2.4 %fusion.1 = f32[2,5,16,16,128]{4,3,2,1,0:T(8,128)} fusion(f32[2,5,16,1,128]{4,3,2,1,0:T(1,128)} %bitcast.22, f32[2,5,16,15,128]{4,3,2,1,0:T(8,128)S(1)} %copy-done.5, f32[2,5,16,15,128]{4,3,2,1,0:T(8,128)S(1)} %copy-done.4, f32[2,5,16,1,128]{4,3,2,1,0:T(1,128)} %bitcast.23), kind=kLoop, calls=%fused_computation.4 | loop fusion | flops 1310720 | bytes 3932160 | tf_op jit(solution)/shard_map/mul | solution.py:165
  70.4 72.2 %scatter.1 = f32[3,256,128]{2,1,0:T(8,128)S(1)} custom-call(f32[32,32,4,128]{3,2,1,0:T(4,128)S(1)} %all-to-all-done.got), custom_call_target="tpu_custom_call" | custom-call | tf_op jit(solution)/shard_map/scatter/pallas_call | solution.py:90
  147.0 2.9 %collective-permute-start = (f32[5,16,1,128]{3,1,2,0:T(8,128)}, f32[5,16,1,128]{3,1,2,0:T(8,128)}, u32[]{:S(2)}, u32[]{:S(2)}) collective-permute-start(f32[5,16,1,128]{3,1,2,0:T(8,128)} %slice.255), channel_id=1, source_target_pairs={{4,0},{8,4},{12,8},{16,12},{20,16},{24,20},{28,24},{5,1},{9,5},{13... | collective-permute-start | bytes 122888 | tf_op jit(solution)/shard_map/ppermute | solution.py:14
  150.6 2.9 %collective-permute-start.1 = (f32[5,16,1,128]{3,1,2,0:T(8,128)}, f32[5,16,1,128]{3,1,2,0:T(8,128)}, u32[]{:S(2)}, u32[]{:S(2)}) collective-permute-start(f32[5,16,1,128]{3,1,2,0:T(8,128)} %slice.256), channel_id=1, source_target_pairs={{0,4},{4,8},{8,12},{12,16},{16,20},{20,24},{24,28},{1,5},{5,9},{9,... | collective-permute-start | bytes 122888 | tf_op jit(solution)/shard_map/ppermute | solution.py:19
  153.5 1.1 slice.260
  154.6 2.2 %copy.138 = f32[5,16,16,1]{2,1,3,0:T(8,128)} copy(f32[5,16,16,1]{3,2,1,0:T(8,128)} %slice.260) | data formatting | bytes 10240 | tf_op jit(solution)/shard_map/slice | solution.py:25
  156.9 1.9 collective-permute-start.3
  158.8 1.1 copy.136
  159.9 3.9 %collective-permute-start.2 = (f32[5,16,16,1]{2,1,3,0:T(8,128)}, f32[5,16,16,1]{2,1,3,0:T(8,128)}, u32[]{:S(2)}, u32[]{:S(2)}) collective-permute-start(f32[5,16,16,1]{2,1,3,0:T(8,128)} %copy.136), channel_id=1, source_target_pairs={{1,0},{2,1},{3,2},{5,4},{6,5},{7,6},{9,8},{10,9},{11,10},{13,12},{... | collective-permute-start | bytes 15368 | tf_op jit(solution)/shard_map/ppermute | solution.py:14
  163.9 1.6 copy.148
  165.5 1.6 copy.152
  167.2 1.1 slice.254
  168.3 1.1 slice.258
  169.4 1.0 copy.130
  170.5 1.0 copy.135
  171.5 2.2 %copy.139 = f32[5,16,16,1]{3,2,1,0:T(8,128)} copy(f32[5,16,16,1]{2,1,3,0:T(8,128)} %collective-permute-done.3) | data formatting | bytes 10240 | tf_op jit(solution)/shard_map/ppermute | solution.py:19
  173.7 2.2 %copy.137 = f32[5,16,16,1]{3,2,1,0:T(8,128)} copy(f32[5,16,16,1]{2,1,3,0:T(8,128)} %collective-permute-done.2) | data formatting | bytes 10240 | tf_op jit(solution)/shard_map/ppermute | solution.py:14
  175.9 2.4 %fusion.4 = f32[5,16,16,128]{3,2,1,0:T(8,128)S(1)} fusion(f32[2,16,16,128]{3,2,1,0:T(8,128)S(1)} %broadcast.168, f32[5,16,1,128]{3,2,1,0:T(1,128)} %bitcast.17, f32[5,16,15,128]{3,2,1,0:T(8,128)} %copy.130, f32[5,16,15,128]{3,2,1,0:T(8,128)} %copy.135, f32[5,16,1,128]{3,2,1,0:T(1,128)} %bitcast.19, f32[5,16,16,1]{3,2,1,0:T(8,128)} %copy.137, ...), kind=kLoop, calls=%fused_computation.13 | loop fusion | flops 2457600 | bytes 4456468 | tf_op jit(solution)/shard_map/sub | solution.py:46
  178.6 1.1 copy-done.3
  181.6 3.8 %collective-permute-start.8 = (f32[5,16,1,128]{3,1,2,0:T(8,128)}, f32[5,16,1,128]{3,1,2,0:T(8,128)}, u32[]{:S(2)}, u32[]{:S(2)}) collective-permute-start(f32[5,16,1,128]{3,1,2,0:T(8,128)} %slice.270), channel_id=1, source_target_pairs={{4,0},{8,4},{12,8},{16,12},{20,16},{24,20},{28,24},{5,1},{9,5},{13... | collective-permute-start | bytes 122888 | tf_op jit(solution)/shard_map/ppermute | solution.py:14
  186.0 2.0 collective-permute-start.9
  188.3 1.1 copy.158
  189.4 2.0 collective-permute-start.11
  191.5 1.2 copy.156
  192.6 3.6 %collective-permute-start.10 = (f32[5,16,16,1]{2,1,3,0:T(8,128)}, f32[5,16,16,1]{2,1,3,0:T(8,128)}, u32[]{:S(2)}, u32[]{:S(2)}) collective-permute-start(f32[5,16,16,1]{2,1,3,0:T(8,128)} %copy.156), channel_id=1, source_target_pairs={{1,0},{2,1},{3,2},{5,4},{6,5},{7,6},{9,8},{10,9},{11,10},{13,12},{... | collective-permute-start | bytes 15368 | tf_op jit(solution)/shard_map/ppermute | solution.py:14
  197.0 2.2 %copy.159 = f32[5,16,16,1]{3,2,1,0:T(8,128)} copy(f32[5,16,16,1]{2,1,3,0:T(8,128)} %collective-permute-done.11) | data formatting | bytes 10240 | tf_op jit(solution)/shard_map/ppermute | solution.py:19
  199.2 2.2 %copy.157 = f32[5,16,16,1]{3,2,1,0:T(8,128)} copy(f32[5,16,16,1]{2,1,3,0:T(8,128)} %collective-permute-done.10) | data formatting | bytes 10240 | tf_op jit(solution)/shard_map/ppermute | solution.py:14
  201.4 2.8 %fusion.5 = f32[5,16,16,128]{3,2,1,0:T(8,128)} fusion(f32[2,16,16,128]{3,2,1,0:T(8,128)S(1)} %broadcast.168, f32[5,16,1,128]{3,2,1,0:T(1,128)} %bitcast.33, f32[5,16,15,128]{3,2,1,0:T(8,128)S(1)} %copy.150, f32[5,16,15,128]{3,2,1,0:T(8,128)S(1)} %copy.155, f32[5,16,1,128]{3,2,1,0:T(1,128)} %bitcast.35, f32[5,16,16,1]{3,2,1,0:T(8,128)} %copy.157, ...), kind=kLoop, calls=%fused_computation.14 | loop fusion | flops 2457600 | bytes 4456468 | tf_op jit(solution)/shard_map/sub | solution.py:46
  (99 shorter events, 15.1 us)
Async XLA Ops:
  0.0 5.0 %copy-start.24 = (f32[512,128]{1,0:T(8,128)S(1)}, f32[512,128]{1,0:T(8,128)}, u32[]{:S(2)}) copy-start(f32[512,128]{1,0:T(8,128)} %param.10) | copy-start | bytes 786436
  2.3 3.7 %copy-start.23 = (f32[512,128]{1,0:T(8,128)S(1)}, f32[512,128]{1,0:T(8,128)}, u32[]{:S(2)}) copy-start(f32[512,128]{1,0:T(8,128)} %param.11) | copy-start | bytes 786436
  10.8 1.4 copy-start
  12.2 5.9 %copy-start.1 = (f32[2,5,16,16,128]{4,3,2,1,0:T(8,128)S(1)}, f32[2,5,16,16,128]{4,3,2,1,0:T(8,128)}, u32[]{:S(2)}) copy-start(f32[2,5,16,16,128]{4,3,2,1,0:T(8,128)} %param.8) | copy-start | bytes 3932164
  12.2 58.2 %all-to-all-start = ((f32[32,32,4,128]{3,2,1,0:T(4,128)}), f32[32,32,4,128]{3,2,1,0:T(4,128)S(1)}, u32[]{:S(2)}, u32[]{:S(2)}) async-start(f32[32,32,4,128]{3,2,1,0:T(4,128)} %bitcast.100), calls=%async_computation | async-start | bytes 4194304 | tf_op jit(solution)/shard_map/all_to_all | solution.py:153
  23.0 20.5 %collective-permute-start.6 = (f32[2,5,16,16,1]{3,2,4,1,0:T(8,128)}, f32[2,5,16,16,1]{3,2,4,1,0:T(8,128)}, u32[]{:S(2)}, u32[]{:S(2)}) collective-permute-start(f32[2,5,16,16,1]{3,2,4,1,0:T(8,128)} %copy.164), channel_id=1, source_target_pairs={{1,0},{2,1},{3,2},{5,4},{6,5},{7,6},{9,8},{10,9},{11,10},{13,12},{... | collective-permute-start | bytes 30728 | tf_op jit(solution)/shard_map/ppermute | solution.py:14
  28.1 18.3 %collective-permute-start.7 = (f32[2,5,16,16,1]{3,2,4,1,0:T(8,128)}, f32[2,5,16,16,1]{3,2,4,1,0:T(8,128)}, u32[]{:S(2)}, u32[]{:S(2)}) collective-permute-start(f32[2,5,16,16,1]{3,2,4,1,0:T(8,128)} %copy.165), channel_id=1, source_target_pairs={{0,1},{1,2},{2,3},{4,5},{5,6},{6,7},{8,9},{9,10},{10,11},{12,13},{... | collective-permute-start | bytes 30728 | tf_op jit(solution)/shard_map/ppermute | solution.py:19
  31.6 34.1 %collective-permute-start.4 = (f32[2,5,16,1,128]{4,2,3,1,0:T(8,128)}, f32[2,5,16,1,128]{4,2,3,1,0:T(8,128)}, u32[]{:S(2)}, u32[]{:S(2)}) collective-permute-start(f32[2,5,16,1,128]{4,2,3,1,0:T(8,128)} %bitcast.47), channel_id=1, source_target_pairs={{4,0},{8,4},{12,8},{16,12},{20,16},{24,20},{28,24},{5,1},{9,5},{13... | collective-permute-start | bytes 245768 | tf_op jit(solution)/shard_map/ppermute | solution.py:14
  35.0 33.0 %collective-permute-start.5 = (f32[2,5,16,1,128]{4,2,3,1,0:T(8,128)S(1)}, f32[2,5,16,1,128]{4,2,3,1,0:T(8,128)}, u32[]{:S(2)}, u32[]{:S(2)}) collective-permute-start(f32[2,5,16,1,128]{4,2,3,1,0:T(8,128)S(1)} %bitcast.118), channel_id=1, source_target_pairs={{0,4},{4,8},{8,12},{12,16},{16,20},{20,24},{24,28},{1,5},{5,9},{9,... | collective-permute-start | bytes 245768 | tf_op jit(solution)/shard_map/ppermute | solution.py:19
  49.4 18.6 %copy-start.4 = (f32[2,5,16,15,128]{4,3,2,1,0:T(8,128)S(1)}, f32[2,5,16,15,128]{4,3,2,1,0:T(8,128)}, u32[]{:S(2)}) copy-start(f32[2,5,16,15,128]{4,3,2,1,0:T(8,128)} %get-tuple-element.23) | copy-start | bytes 3686404
  49.4 18.6 %copy-start.5 = (f32[2,5,16,15,128]{4,3,2,1,0:T(8,128)S(1)}, f32[2,5,16,15,128]{4,3,2,1,0:T(8,128)}, u32[]{:S(2)}) copy-start(f32[2,5,16,15,128]{4,3,2,1,0:T(8,128)} %get-tuple-element.24) | copy-start | bytes 3686404
  70.4 72.2 %copy-start.14 = (f32[5,16,16,128]{3,2,1,0:T(8,128)S(1)}, f32[5,16,16,128]{3,2,1,0:T(8,128)}, u32[]{:S(2)}) copy-start(f32[5,16,16,128]{3,2,1,0:T(8,128)} %param.7) | copy-start | bytes 1966084
  142.6 1.3 copy-start.6
  142.7 1.6 copy-start.2
  142.8 1.6 copy-start.17
  142.8 1.6 copy-start.18
  144.4 0.9 copy-start.20
  144.4 1.0 copy-start.22
  145.6 0.8 copy-start.9
  145.6 4.4 %copy-start.10 = (f32[5,16,16,128]{3,1,2,0:T(8,128)}, f32[5,16,16,128]{3,1,2,0:T(8,128)S(1)}, u32[]{:S(2)}) copy-start(f32[5,16,16,128]{3,1,2,0:T(8,128)S(1)} %get-tuple-element.33) | copy-start | bytes 1966084
  147.0 28.9 %collective-permute-start = (f32[5,16,1,128]{3,1,2,0:T(8,128)}, f32[5,16,1,128]{3,1,2,0:T(8,128)}, u32[]{:S(2)}, u32[]{:S(2)}) collective-permute-start(f32[5,16,1,128]{3,1,2,0:T(8,128)} %slice.255), channel_id=1, source_target_pairs={{4,0},{8,4},{12,8},{16,12},{20,16},{24,20},{28,24},{5,1},{9,5},{13... | collective-permute-start | bytes 122888 | tf_op jit(solution)/shard_map/ppermute | solution.py:14
  150.6 25.3 %collective-permute-start.1 = (f32[5,16,1,128]{3,1,2,0:T(8,128)}, f32[5,16,1,128]{3,1,2,0:T(8,128)}, u32[]{:S(2)}, u32[]{:S(2)}) collective-permute-start(f32[5,16,1,128]{3,1,2,0:T(8,128)} %slice.256), channel_id=1, source_target_pairs={{0,4},{4,8},{8,12},{12,16},{16,20},{20,24},{24,28},{1,5},{5,9},{9,... | collective-permute-start | bytes 122888 | tf_op jit(solution)/shard_map/ppermute | solution.py:19
  156.9 14.7 %collective-permute-start.3 = (f32[5,16,16,1]{2,1,3,0:T(8,128)}, f32[5,16,16,1]{2,1,3,0:T(8,128)}, u32[]{:S(2)}, u32[]{:S(2)}) collective-permute-start(f32[5,16,16,1]{2,1,3,0:T(8,128)} %copy.138), channel_id=1, source_target_pairs={{0,1},{1,2},{2,3},{4,5},{5,6},{6,7},{8,9},{9,10},{10,11},{12,13},{... | collective-permute-start | bytes 15368 | tf_op jit(solution)/shard_map/ppermute | solution.py:19
  159.9 8.4 %copy-start.11 = (f32[5,16,16,128]{3,1,2,0:T(8,128)S(1)}, f32[5,16,16,128]{3,1,2,0:T(8,128)}, u32[]{:S(2)}) copy-start(f32[5,16,16,128]{3,1,2,0:T(8,128)} %copy-done.10) | copy-start | bytes 1966084
  159.9 13.8 %collective-permute-start.2 = (f32[5,16,16,1]{2,1,3,0:T(8,128)}, f32[5,16,16,1]{2,1,3,0:T(8,128)}, u32[]{:S(2)}, u32[]{:S(2)}) collective-permute-start(f32[5,16,16,1]{2,1,3,0:T(8,128)} %copy.136), channel_id=1, source_target_pairs={{1,0},{2,1},{3,2},{5,4},{6,5},{7,6},{9,8},{10,9},{11,10},{13,12},{... | collective-permute-start | bytes 15368 | tf_op jit(solution)/shard_map/ppermute | solution.py:14
  170.5 5.4 %copy-start.8 = (f32[5,16,16,127]{3,2,1,0:T(8,128)S(1)}, f32[5,16,16,127]{3,2,1,0:T(8,128)}, u32[]{:S(2)}) copy-start(f32[5,16,16,127]{3,2,1,0:T(8,128)} %slice.258) | copy-start | bytes 1950724
  175.9 2.7 %copy-start.7 = (f32[2,5,16,16,128]{4,3,2,1,0:T(8,128)S(1)}, f32[2,5,16,16,128]{4,3,2,1,0:T(8,128)}, u32[]{:S(2)}) copy-start(f32[2,5,16,16,128]{4,3,2,1,0:T(8,128)} %fusion.2) | copy-start | bytes 3932164
  178.3 1.3 copy-start.3
  178.3 1.3 copy-start.15
  178.4 1.3 copy-start.16
  179.7 1.0 copy-start.19
  179.7 1.0 copy-start.21
  180.9 7.1 %copy-start.12 = (f32[5,16,16,128]{3,1,2,0:T(8,128)}, f32[5,16,16,128]{3,1,2,0:T(8,128)S(1)}, u32[]{:S(2)}) copy-start(f32[5,16,16,128]{3,1,2,0:T(8,128)S(1)} %get-tuple-element.28) | copy-start | bytes 1966084
  181.6 19.8 %collective-permute-start.8 = (f32[5,16,1,128]{3,1,2,0:T(8,128)}, f32[5,16,1,128]{3,1,2,0:T(8,128)}, u32[]{:S(2)}, u32[]{:S(2)}) collective-permute-start(f32[5,16,1,128]{3,1,2,0:T(8,128)} %slice.270), channel_id=1, source_target_pairs={{4,0},{8,4},{12,8},{16,12},{20,16},{24,20},{28,24},{5,1},{9,5},{13... | collective-permute-start | bytes 122888 | tf_op jit(solution)/shard_map/ppermute | solution.py:14
  186.0 15.4 %collective-permute-start.9 = (f32[5,16,1,128]{3,1,2,0:T(8,128)}, f32[5,16,1,128]{3,1,2,0:T(8,128)}, u32[]{:S(2)}, u32[]{:S(2)}) collective-permute-start(f32[5,16,1,128]{3,1,2,0:T(8,128)} %slice.271), channel_id=1, source_target_pairs={{0,4},{4,8},{8,12},{12,16},{16,20},{20,24},{24,28},{1,5},{5,9},{9,... | collective-permute-start | bytes 122888 | tf_op jit(solution)/shard_map/ppermute | solution.py:19
  189.4 6.9 %copy-start.13 = (f32[5,16,16,128]{3,1,2,0:T(8,128)S(1)}, f32[5,16,16,128]{3,1,2,0:T(8,128)}, u32[]{:S(2)}) copy-start(f32[5,16,16,128]{3,1,2,0:T(8,128)} %copy-done.12) | copy-start | bytes 1966084
  189.4 7.6 %collective-permute-start.11 = (f32[5,16,16,1]{2,1,3,0:T(8,128)}, f32[5,16,16,1]{2,1,3,0:T(8,128)}, u32[]{:S(2)}, u32[]{:S(2)}) collective-permute-start(f32[5,16,16,1]{2,1,3,0:T(8,128)} %copy.158), channel_id=1, source_target_pairs={{0,1},{1,2},{2,3},{4,5},{5,6},{6,7},{8,9},{9,10},{10,11},{12,13},{... | collective-permute-start | bytes 15368 | tf_op jit(solution)/shard_map/ppermute | solution.py:19
  192.6 6.6 %collective-permute-start.10 = (f32[5,16,16,1]{2,1,3,0:T(8,128)}, f32[5,16,16,1]{2,1,3,0:T(8,128)}, u32[]{:S(2)}, u32[]{:S(2)}) collective-permute-start(f32[5,16,16,1]{2,1,3,0:T(8,128)} %copy.156), channel_id=1, source_target_pairs={{1,0},{2,1},{3,2},{5,4},{6,5},{7,6},{9,8},{10,9},{11,10},{13,12},{... | collective-permute-start | bytes 15368 | tf_op jit(solution)/shard_map/ppermute | solution.py:14
